TPU v7x, 128 devices: a whole 4x4x4 slice. The times are simulated.
128 devices in a mesh: prow: 8 (over x, core), pcol: 16 (over y, z).
Axes of the slice: x: 4, y: 4, z: 4, core: 2. Of those that a mesh axis runs over, the one named last changes fastest.
Arguments:
- front: float32 [59, 8, 128, 1, 16, 128], P(None, 'prow', None, None, 'pcol'), may hold values from -66 to 396
- child: float32 [2, 8, 8, 128, 16, 128], P(None, None, 'prow', None, 'pcol'), may hold values from -6 to 6
- row_map: int32 [2, 64], replicated, may hold values from 0 to 471, as said below
- col_map: int32 [2, 16], replicated, may hold values from 0 to 15, as said below
Outputs:
- factor: float32 [59, 8, 128, 1, 16, 128], P(None, 'prow', None, None, 'pcol')
Inputs may be any that keep to these rules, and one draw needn't show every extreme that they name: Within one child all entries differ. For each child c and each index p of prow, the entries row_map[c, l * 8 + p] for l = 0 .. 7 have different remainders modulo 8. `col_map`: within one child all entries differ.
All inputs are finite; a program needn't handle non-finite values.
Results may differ from a plain program's by a relative error of at most 0.0001.
Values sent between devices are 32-bit elements; how exact they have to be, the bound alone decides.
No kernel may reach another device: no remote copies, remote signals or barrier semaphores. Data moves between devices by JAX's collectives and lax.ppermute only.
A program may use at most 128 MiB of HBM per device.

v0:
```python
import jax
import jax.numpy as jnp
from jax import lax
from jax.sharding import PartitionSpec as P

HIGHEST_PRECISION = lax.Precision.HIGHEST


def broadcast(block, axis, holder):
    block = jnp.where(lax.axis_index(axis) == holder, block, jnp.zeros_like(block))
    return lax.psum(block, axis)


def spread(strip, root):
    return broadcast(strip, "pcol", root)


def sort_by_owner(blocks, owners, prow_count):
    choose = (owners[:, None, :] == jnp.arange(prow_count)[None, :, None]).astype(jnp.float32)
    return jnp.einsum("cdl,clrx->cdrx", choose, blocks, precision=HIGHEST_PRECISION)


def place_columns(carry, piece, col_map, col_here, pcol_count, block_size):
    count = piece.shape[3] // block_size
    target = jnp.arange(carry.shape[3]) * pcol_count + col_here
    pick = (col_map[:, :, None] == target[None, None, :]).astype(jnp.float32)
    shaped = piece.reshape(piece.shape[0], piece.shape[1], block_size, count, block_size)
    return jnp.einsum("csrtk,ctm->csrmk", shaped, pick, precision=HIGHEST_PRECISION)


def on_device(front, child, row_map, col_map):
    row_blocks = front.shape[0]
    block_size = front.shape[2]
    col_blocks = front.shape[3]
    prow_count = lax.axis_size("prow")
    pcol_count = lax.axis_size("pcol")
    row_here = lax.axis_index("prow")
    col_here = lax.axis_index("pcol")
    local_rows = child.shape[1]
    matrix = front.reshape(row_blocks * block_size, col_blocks * block_size)
    table = row_map.reshape(2, local_rows, prow_count)
    owners = (
        jnp.sum(jnp.where(jnp.arange(prow_count)[None, None, :] == row_here, table, 0), axis=2)
        % prow_count
    )
    arrival = jnp.sum(jnp.where(table % prow_count == row_here, table // prow_count, 0), axis=1)
    raw = child.reshape(2, local_rows, block_size, block_size)
    moved = lax.all_to_all(
        sort_by_owner(raw, owners, prow_count), "prow", split_axis=1, concat_axis=1, tiled=True
    )
    empty = jnp.zeros((2, prow_count, block_size, col_blocks, block_size), jnp.float32)
    placed = place_columns(
        empty,
        lax.all_gather(moved, "pcol", axis=3, tiled=True),
        col_map,
        col_here,
        pcol_count,
        block_size,
    )
    arrived = placed.reshape(2, prow_count, block_size, col_blocks * block_size)
    stacked = matrix.reshape(row_blocks, block_size, col_blocks * block_size)
    for member in range(2):
        stacked = stacked.at[arrival[member]].add(arrived[member])
    matrix = stacked.reshape(row_blocks * block_size, col_blocks * block_size)
    row_ids = (
        (jnp.arange(row_blocks)[:, None] * prow_count + row_here) * block_size
        + jnp.arange(block_size)[None, :]
    ).reshape(-1)
    col_ids = (
        (jnp.arange(col_blocks)[:, None] * pcol_count + col_here) * block_size
        + jnp.arange(block_size)[None, :]
    ).reshape(-1)
    for segment in range(2):
        start_col = 2 * segment * block_size
        stop_col = start_col + 2 * block_size
        strips = [spread(matrix, 2 * segment + member) for member in range(2)]
        panel = jnp.concatenate(strips, axis=1)
        wanted = [jnp.int32(2 * segment), jnp.int32(2 * segment + 1)]
        wanted = wanted + [col_here + 0]
        pieces = []
        for target in wanted:
            section = lax.dynamic_slice_in_dim(
                panel, target // prow_count * block_size, block_size, 0
            )
            pieces.append(jnp.where(target % prow_count == row_here, section, 0.0))
        gathered = lax.psum(jnp.concatenate(pieces, axis=0), "prow")
        diag = gathered[: 2 * block_size]
        sym = jnp.tril(diag) + jnp.tril(diag, -1).T
        lower = jnp.linalg.cholesky(sym)
        inverse = lax.linalg.triangular_solve(
            lower, jnp.eye(2 * block_size, dtype=jnp.float32), left_side=True, lower=True
        )
        factor = jnp.dot(panel, inverse.T, precision=HIGHEST_PRECISION)
        col_factor = jnp.dot(gathered[2 * block_size :], inverse.T, precision=HIGHEST_PRECISION)
        shaped = factor.reshape(row_blocks, block_size, 2 * block_size)
        for member in range(2):
            target = 2 * segment + member
            slot = target // prow_count
            replaced = jnp.where(
                row_here == target % prow_count,
                lower[member * block_size : (member + 1) * block_size],
                shaped[slot],
            )
            shaped = shaped.at[slot].set(replaced)
        factor = shaped.reshape(row_blocks * block_size, 2 * block_size)
        for member in range(2):
            owned = col_here == 2 * segment + member
            written = jnp.where(
                owned, factor[:, member * block_size : (member + 1) * block_size], matrix
            )
            matrix = matrix.at[:, :block_size].set(written)
        change = jnp.dot(factor, col_factor.T, precision=HIGHEST_PRECISION)
        matrix = matrix - jnp.where(col_ids[None, :] >= stop_col, change, 0.0)
    keep = row_ids[:, None] >= jnp.minimum(col_ids, 4 * block_size)[None, :]
    return jnp.where(keep, matrix, 0.0).reshape(front.shape)


def solution(mesh):
    return jax.shard_map(
        on_device,
        mesh=mesh,
        in_specs=(
            P(None, "prow", None, None, "pcol", None),
            P(None, None, "prow", None, "pcol", None),
            P(),
            P(),
        ),
        out_specs=P(None, "prow", None, None, "pcol", None),
        check_vma=False,
    )
```

profile of v0, /device:TPU:0, one launch (start us, length us, event | category | flops | bytes accessed | tf_op | source)
XLA Modules:
  0.0 761.4 jit_solution(10043648452690605606)
XLA Ops:
  6.5 4.5 copy.75
  12.7 20.4 %all_to_all.5 = f32[2,8,128,128]{3,2,0,1:T(8,128)} all-to-all(f32[2,8,128,128]{3,2,0,1:T(8,128)S(1)} %copy.14), channel_id=1, replica_groups=mesh['prow'=8,'pcol'=16] {'prow'}, dimensions={1} | all-to-all | bytes 2097152 | tf_op jit(solution)/shard_map/all_to_all | solution.py:48
  33.2 121.8 %all-gather.2.cloned.1.call-done = f32[2,8,128,2048]{3,2,0,1:T(8,128)} async-done(((f32[2,8,128,128]{3,2,0,1:T(8,128)}), f32[2,8,128,2048]{3,2,0,1:T(8,128)}) %all-gather.2.cloned.1.call-update) | async-done | bytes 16777232 | tf_op jit(solution)/shard_map/all_gather | solution.py:54
  155.0 9.4 %copy.32 = f32[256,8,16,128]{3,2,1,0:T(8,128)S(1)} copy(f32[256,8,16,128]{3,1,2,0:T(8,128)} %bitcast.134) | data formatting | bytes 33554432
  164.4 6.5 fusion
  171.0 2.7 scatter_fusion
  173.7 2.7 scatter_fusion.1
  176.4 5.7 bitcast_select_fusion
  182.2 134.7 %all-reduce.14.cloned.1.call-done = (f32[7552,128]{1,0:T(8,128)}, f32[7552,128]{1,0:T(8,128)}) async-done(((f32[7552,128]{1,0:T(8,128)}, f32[7552,128]{1,0:T(8,128)}), (f32[7552,128]{1,0:T(8,128)}, f32[7552,128]{1,0:T(8,128)})) %all-reduce.14.cloned.1.call-update) | async-done | bytes 7733264 | tf_op jit(solution)/shard_map/psum | solution.py:11
  316.9 2.5 constant_dynamic-update-slice_fusion.1
  320.5 3.0 copy-done.3
  324.7 59.9 %all-reduce.8.cloned.1.call-done = f32[384,256]{1,0:T(8,128)} async-done(((f32[384,256]{1,0:T(8,128)}), f32[384,256]{1,0:T(8,128)}) %all-reduce.8.cloned.1.call-update) | async-done | bytes 393232 | tf_op jit(solution)/shard_map/psum | solution.py:86
  387.0 11.7 %cholesky.130 = f32[128,128]{1,0:T(8,128)S(1)} custom-call(f32[128,128]{1,0:T(8,128)S(1)} %cholesky.194), custom_call_target="Cholesky" | custom-call | tf_op jit(solution)/shard_map/jit(cholesky)/cholesky | solution.py:89
  398.7 9.8 %custom-call.13 = f32[1,128,128]{1,2,0:T(8,128)S(1)} custom-call(f32[1,128,128]{2,1,0:T(8,128)S(1)} %get-tuple-element.200), custom_call_target="InvertDiagBlocksLowerTriangular" | custom-call | tf_op jit(solution)/shard_map/jit(cholesky)/cholesky | solution.py:89
  409.0 11.7 %cholesky.147 = f32[128,128]{1,0:T(8,128)S(1)} custom-call(f32[128,128]{1,0:T(8,128)S(1)} %convolution_subtract_fusion.3), custom_call_target="Cholesky" | custom-call | tf_op jit(solution)/shard_map/jit(cholesky)/cholesky | solution.py:89
  422.9 4.3 while.16
  427.2 19.7 %custom-call.14 = f32[2,128,128]{1,2,0:T(8,128)S(1)} custom-call(f32[2,128,128]{2,1,0:T(8,128)S(1)} %get-tuple-element.149), custom_call_target="InvertDiagBlocksLowerTriangular" | custom-call | tf_op jit(solution)/shard_map/triangular_solve/custom-call.0 | solution.py:90
  447.8 9.0 %fusion.18 = f32[7552,256]{1,0:T(8,128)S(1)} fusion(f32[7552,256]{1,0:T(8,128)} %copy-done.3, f32[128,256]{1,0:T(8,128)S(1)} %fusion.34, f32[128,256]{1,0:T(8,128)S(1)} %fusion.27), kind=kOutput, calls=%fused_computation.52 | convolution fusion | flops 5939200000 | bytes 15728640 | tf_op jit(solution)/shard_map/dot_general | solution.py:93
  457.7 1.5 fusion.17
  459.2 9.2 %broadcast_select_fusion = (f32[7552,128]{1,0:T(8,128)}, f32[7552,128]{1,0:T(8,128)}, f32[7552,128]{1,0:T(8,128)}) fusion(pred[]{:T(512)S(6)} %eq.100, pred[]{:T(512)S(6)} %eq.101, f32[7552,256]{1,0:T(8,128)S(1)} %bitcast.132, f32[128,256]{1,0:T(8,128)S(1)} %fusion.17, pred[128]{0:T(512)(128)(4,1)S(1)} %fusion.52, f32[7552,128]{1,0:T(8,128)S(1)} %bitcast.131, ...), kind=kOutput, calls=%fused_computation.19 | convolution fusion | flops 2975367168 | bytes 31064580 | tf_op jit(solution)/shard_map/dot_general | solution.py:112
  469.2 134.1 %all-reduce.12.cloned.1.call-done = (f32[7552,128]{1,0:T(8,128)}, f32[7552,128]{1,0:T(8,128)}) async-done(((f32[7552,128]{1,0:T(8,128)}, f32[7552,128]{1,0:T(8,128)}), (f32[7552,128]{1,0:T(8,128)}, f32[7552,128]{1,0:T(8,128)})) %all-reduce.12.cloned.1.call-update) | async-done | bytes 7733264 | tf_op jit(solution)/shard_map/psum | solution.py:11
  603.3 2.5 constant_dynamic-update-slice_fusion.3
  606.8 3.0 copy-done.4
  610.8 60.1 %all-reduce.10.cloned.1.call-done = f32[384,256]{1,0:T(8,128)} async-done(((f32[384,256]{1,0:T(8,128)}), f32[384,256]{1,0:T(8,128)}) %all-reduce.10.cloned.1.call-update) | async-done | bytes 393232 | tf_op jit(solution)/shard_map/psum | solution.py:86
  673.3 11.7 %cholesky.164 = f32[128,128]{1,0:T(8,128)S(1)} custom-call(f32[128,128]{1,0:T(8,128)S(1)} %cholesky.197), custom_call_target="Cholesky" | custom-call | tf_op jit(solution)/shard_map/jit(cholesky)/cholesky | solution.py:89
  685.0 9.8 %custom-call.15 = f32[1,128,128]{1,2,0:T(8,128)S(1)} custom-call(f32[1,128,128]{2,1,0:T(8,128)S(1)} %get-tuple-element.196), custom_call_target="InvertDiagBlocksLowerTriangular" | custom-call | tf_op jit(solution)/shard_map/jit(cholesky)/cholesky | solution.py:89
  695.3 11.7 %cholesky.181 = f32[128,128]{1,0:T(8,128)S(1)} custom-call(f32[128,128]{1,0:T(8,128)S(1)} %convolution_subtract_fusion.2), custom_call_target="Cholesky" | custom-call | tf_op jit(solution)/shard_map/jit(cholesky)/cholesky | solution.py:89
  709.9 4.3 while.17
  714.1 19.7 %custom-call.16 = f32[2,128,128]{1,2,0:T(8,128)S(1)} custom-call(f32[2,128,128]{2,1,0:T(8,128)S(1)} %get-tuple-element.150), custom_call_target="InvertDiagBlocksLowerTriangular" | custom-call | tf_op jit(solution)/shard_map/triangular_solve/custom-call.0 | solution.py:90
  734.7 8.5 %fusion.16 = f32[7552,256]{1,0:T(8,128)S(1)} fusion(f32[7552,256]{1,0:T(8,128)} %copy-done.4, f32[128,256]{1,0:T(8,128)S(1)} %fusion.30, f32[128,256]{1,0:T(8,128)S(1)} %fusion.25), kind=kOutput, calls=%fused_computation.50 | convolution fusion | flops 5939200000 | bytes 15728640 | tf_op jit(solution)/shard_map/dot_general | solution.py:93
  744.3 1.5 fusion.15
  745.8 8.9 %fusion.4 = f32[7552,128]{1,0:T(8,128)} fusion(f32[7552,256]{1,0:T(8,128)S(1)} %bitcast.133, f32[128,256]{1,0:T(8,128)S(1)} %fusion.15, f32[7552,128]{1,0:T(8,128)S(1)} %copy-done.5, s32[128]{0:T(128)S(1)} %fusion.53, s32[7552]{0:T(1024)S(1)} %add_bitcast_fusion, pred[128]{0:T(512)(128)(4,1)S(1)} %fusion.51, pred[]{:T(512)S(6)} %eq.101, pred[]{:T(512)S(6)} %eq.100), kind=kOutput, calls=%fused_computation.12 | convolution fusion | flops 2975367168 | bytes 23364610 | tf_op jit(solution)/shard_map/dot_general | solution.py:112
  (107 shorter events, 26.3 us)
Async XLA Ops:
  6.5 4.8 copy-start
  6.5 4.6 copy-start.8
  6.5 26.7 %copy-start.9 = (s32[2,16]{1,0:T(2,128)S(1)}, s32[2,16]{1,0:T(2,128)}, u32[]{:S(2)}) copy-start(s32[2,16]{1,0:T(2,128)} %param.34) | copy-start | bytes 388
  6.5 148.5 %all-gather.2.cloned.1.call-start = ((), (), s32[]{:S(2)}) async-start(), calls=%async_computation.1 | async-start | bytes 17825792 | tf_op jit(solution)/shard_map/all_gather | solution.py:54
  33.2 283.8 %all-reduce.14.cloned.1.call-start = ((), (), s32[]{:S(2)}) async-start(), calls=%async_computation.5 | async-start | bytes 15466496 | tf_op jit(solution)/shard_map/psum | solution.py:11
  182.1 202.5 %all-reduce.8.cloned.1.call-start = ((), (), s32[]{:S(2)}) async-start(), calls=%async_computation.2 | async-start | bytes 786432 | tf_op jit(solution)/shard_map/psum | solution.py:86
  316.9 3.3 copy-start.6
  320.5 3.1 copy-start.3
  324.4 278.9 %all-reduce.12.cloned.1.call-start = ((), (), s32[]{:S(2)}) async-start(), calls=%async_computation.4 | async-start | bytes 15466496 | tf_op jit(solution)/shard_map/psum | solution.py:11
  456.8 2.5 copy-start.2
  468.4 202.5 %all-reduce.10.cloned.1.call-start = ((), (), s32[]{:S(2)}) async-start(), calls=%async_computation.3 | async-start | bytes 786432 | tf_op jit(solution)/shard_map/psum | solution.py:86
  603.3 3.3 copy-start.7
  606.8 3.1 copy-start.4
  743.3 2.5 copy-start.5
  745.7 9.0 %copy-start.1 = (f32[2,8,1,128,1,128]{5,4,3,2,1,0:T(1,128)S(1)}, f32[2,8,1,128,1,128]{5,4,3,2,1,0:T(1,128)}, u32[]{:S(2)}) copy-start(f32[2,8,1,128,1,128]{5,4,3,2,1,0:T(1,128)} %param.32) | copy-start | bytes 3145732
Sparse Core Ops, SparseCore 0:
  33.3 121.7 all-gather.1
  182.2 134.6 all-reduce.13
  324.5 60.0 all-reduce.7
  468.6 134.6 all-reduce.11
  610.8 60.0 all-reduce.9
where the time goes:
time: 769 us; the launch traced here: 761 us
  waiting for transfers between devices  511 us (66%)
  other arithmetic  124 us (16%)
  matrix products  49 us (6%)
  local copies, waits for them, and re-layouts  39.2 us (5%)
  blocking collectives  20.4 us (3%)
  between operations  16.6 us (2%)
    psum x2, waiting for transfers between devices, broadcast(): return lax.psum(block, axis)  269 us
    all_gather x1, waiting for transfers between devices, on_device(): lax.all_gather(moved, 'pcol', axis=3, tiled=True)  122 us
    psum x2, waiting for transfers between devices, on_device(): gathered = lax.psum(jnp.concatenate(pieces, axis=0), 'prow')  120 us
    another operation x13, other arithmetic, on_device(): lower = jnp.linalg.cholesky(sym)  68.7 us
    another operation x5, other arithmetic, on_device(): lax.linalg.triangular_solve(lower, jnp.eye(2 * block_size, dtype=jnp.floa...  39.4 us
    unnamed x26, local copies, waits for them, and re-layouts  28.4 us
    all_to_all x1, blocking collectives, on_device(): lax.all_to_all(sort_by_owner(raw, owners, prow_count), 'prow', split_axis...  20.4 us
    dot_general x2, matrix products, on_device(): change = jnp.dot(factor, col_factor.T, precision=HIGHEST_PRECISION)  18.1 us
  transfers between devices with their start and end apart: 5, of which 5 were waited for; matrix products, arithmetic and copies ran while one was open for 0% of the time, Pallas kernels for 0%

commit v1 on v0

--- a/solution.py
+++ b/solution.py
@@ -51,7 +51,9 @@
     empty = jnp.zeros((2, prow_count, block_size, col_blocks, block_size), jnp.float32)
     placed = place_columns(
         empty,
-        lax.all_gather(moved, "pcol", axis=3, tiled=True),
+        jnp.concatenate(
+            lax.all_to_all(jnp.stack([moved] * lax.axis_size("pcol")), "pcol", 0, 0), axis=3
+        ),
         col_map,
         col_here,
         pcol_count,

time: 769 us -> 961 us (1.25)
  waiting for transfers between devices: 511 us -> 686 us
  matrix products: 49 us -> 63.1 us
    all_to_all x0 -> x1, waiting for transfers between devices: none -> 291 us  [on_device(): lax.all_to_all(jnp.stack([moved] * lax.axis_size('pcol')), 'pcol', 0, 0)]
    all_gather x1 -> x0, waiting for transfers between devices: 122 us -> none  [on_device(): lax.all_gather(moved, 'pcol', axis=3, tiled=True)]
    dot_general x1, matrix products: 6.49 us -> 20.6 us  [place_columns(): jnp.einsum('csrtk,ctm->csrmk', shaped, pick, precision=HIGHEST_PRECISION)]
    unnamed x26 -> x25, local copies, waits for them, and re-layouts: 28.4 us -> 19 us
where the time goes in v1:
time: 961 us; the launch traced here: 958 us
  waiting for transfers between devices  686 us (71%)
  other arithmetic  124 us (13%)
  matrix products  63.1 us (7%)
  local copies, waits for them, and re-layouts  37.4 us (4%)
  blocking collectives  20.3 us (2%)
  between operations  16.5 us (2%)
    all_to_all x1, waiting for transfers between devices, on_device(): lax.all_to_all(jnp.stack([moved] * lax.axis_size('pcol')), 'pcol', 0, 0)  291 us
    psum x2, waiting for transfers between devices, broadcast(): return lax.psum(block, axis)  275 us
    psum x2, waiting for transfers between devices, on_device(): gathered = lax.psum(jnp.concatenate(pieces, axis=0), 'prow')  120 us
    another operation x13, other arithmetic, on_device(): lower = jnp.linalg.cholesky(sym)  68.6 us
    another operation x5, other arithmetic, on_device(): lax.linalg.triangular_solve(lower, jnp.eye(2 * block_size, dtype=jnp.floa...  39.4 us
    dot_general x1, matrix products, place_columns(): jnp.einsum('csrtk,ctm->csrmk', shaped, pick, precision=HIGHEST_PRECISION)  20.6 us
    all_to_all x1, blocking collectives, on_device(): lax.all_to_all(sort_by_owner(raw, owners, prow_count), 'prow', split_axis...  20.3 us
  transfers between devices with their start and end apart: 5, of which 5 were waited for; matrix products, arithmetic and copies ran while one was open for 0% of the time, Pallas kernels for 0%

profile of v1, /device:TPU:0, one launch (start us, length us, event | category | flops | bytes accessed | tf_op | source)
XLA Modules:
  0.0 957.6 jit_solution(15405921732672675661)
XLA Ops:
  6.5 4.6 copy.74
  12.7 20.3 %all_to_all.10 = f32[2,8,128,128]{3,2,0,1:T(8,128)S(1)} all-to-all(f32[2,8,128,128]{3,2,0,1:T(8,128)S(1)} %copy.22), channel_id=1, replica_groups=mesh['prow'=8,'pcol'=16] {'prow'}, dimensions={1} | all-to-all | bytes 2097152 | tf_op jit(solution)/shard_map/all_to_all | solution.py:48
  33.1 7.8 stack.2
  41.0 8.2 all-to-all-start.1
  49.5 291.1 %all-to-all-done.1 = f32[16,2,8,128,128]{4,3,2,1,0:T(8,128)} async-done(((f32[16,2,8,128,128]{4,3,2,1,0:T(8,128)}), f32[16,2,8,128,128]{4,3,2,1,0:T(8,128)}, u32[]{:S(2)}, u32[]{:S(2)}) %all-to-all-start.1) | async-done | bytes 16777248 | tf_op jit(solution)/shard_map/all_to_all | solution.py:55
  340.5 20.6 %fusion = f32[2,1,8,128,128]{4,1,3,2,0:T(1,128)S(1)} fusion(f32[2,8,128,16,128]{4,2,1,0,3:T(8,128)} %bitcast.8, pred[2,16,1,1,1]{1,0,2,3,4:T(4,128)(4,1)S(1)} %compare_bitcast_fusion), kind=kOutput, calls=%fused_computation.6 | convolution fusion | flops 50331648 | bytes 17825824 | tf_op jit(solution)/shard_map/csrtk,ctm->csrmk/dot_general | solution.py:28
  361.2 2.7 scatter_fusion
  363.9 2.7 scatter_fusion.1
  366.6 5.7 bitcast_select_fusion
  372.5 140.8 %all-reduce.14.cloned.1.call-done = (f32[7552,128]{1,0:T(8,128)}, f32[7552,128]{1,0:T(8,128)}) async-done(((f32[7552,128]{1,0:T(8,128)}, f32[7552,128]{1,0:T(8,128)}), (f32[7552,128]{1,0:T(8,128)}, f32[7552,128]{1,0:T(8,128)})) %all-reduce.14.cloned.1.call-update) | async-done | bytes 7733264 | tf_op jit(solution)/shard_map/psum | solution.py:11
  513.3 2.5 constant_dynamic-update-slice_fusion.1
  516.9 3.0 copy-done.3
  521.1 59.9 %all-reduce.8.cloned.1.call-done = f32[384,256]{1,0:T(8,128)} async-done(((f32[384,256]{1,0:T(8,128)}), f32[384,256]{1,0:T(8,128)}) %all-reduce.8.cloned.1.call-update) | async-done | bytes 393232 | tf_op jit(solution)/shard_map/psum | solution.py:88
  583.3 11.7 %cholesky.130 = f32[128,128]{1,0:T(8,128)S(1)} custom-call(f32[128,128]{1,0:T(8,128)S(1)} %cholesky.194), custom_call_target="Cholesky" | custom-call | tf_op jit(solution)/shard_map/jit(cholesky)/cholesky | solution.py:91
  595.1 9.8 %custom-call.13 = f32[1,128,128]{1,2,0:T(8,128)S(1)} custom-call(f32[1,128,128]{2,1,0:T(8,128)S(1)} %get-tuple-element.200), custom_call_target="InvertDiagBlocksLowerTriangular" | custom-call | tf_op jit(solution)/shard_map/jit(cholesky)/cholesky | solution.py:91
  605.4 11.7 %cholesky.147 = f32[128,128]{1,0:T(8,128)S(1)} custom-call(f32[128,128]{1,0:T(8,128)S(1)} %convolution_subtract_fusion.3), custom_call_target="Cholesky" | custom-call | tf_op jit(solution)/shard_map/jit(cholesky)/cholesky | solution.py:91
  619.2 4.3 while.16
  623.5 19.7 %custom-call.14 = f32[2,128,128]{1,2,0:T(8,128)S(1)} custom-call(f32[2,128,128]{2,1,0:T(8,128)S(1)} %get-tuple-element.149), custom_call_target="InvertDiagBlocksLowerTriangular" | custom-call | tf_op jit(solution)/shard_map/triangular_solve/custom-call.0 | solution.py:92
  644.1 9.0 fusion.18
  654.1 1.5 fusion.17
  655.6 9.2 broadcast_select_fusion
  665.3 134.3 %all-reduce.12.cloned.1.call-done = (f32[7552,128]{1,0:T(8,128)}, f32[7552,128]{1,0:T(8,128)}) async-done(((f32[7552,128]{1,0:T(8,128)}, f32[7552,128]{1,0:T(8,128)}), (f32[7552,128]{1,0:T(8,128)}, f32[7552,128]{1,0:T(8,128)})) %all-reduce.12.cloned.1.call-update) | async-done | bytes 7733264 | tf_op jit(solution)/shard_map/psum | solution.py:11
  799.6 2.5 constant_dynamic-update-slice_fusion.3
  803.2 3.0 copy-done.4
  807.1 60.1 %all-reduce.10.cloned.1.call-done = f32[384,256]{1,0:T(8,128)} async-done(((f32[384,256]{1,0:T(8,128)}), f32[384,256]{1,0:T(8,128)}) %all-reduce.10.cloned.1.call-update) | async-done | bytes 393232 | tf_op jit(solution)/shard_map/psum | solution.py:88
  869.6 11.7 %cholesky.164 = f32[128,128]{1,0:T(8,128)S(1)} custom-call(f32[128,128]{1,0:T(8,128)S(1)} %cholesky.197), custom_call_target="Cholesky" | custom-call | tf_op jit(solution)/shard_map/jit(cholesky)/cholesky | solution.py:91
  881.4 9.8 %custom-call.15 = f32[1,128,128]{1,2,0:T(8,128)S(1)} custom-call(f32[1,128,128]{2,1,0:T(8,128)S(1)} %get-tuple-element.196), custom_call_target="InvertDiagBlocksLowerTriangular" | custom-call | tf_op jit(solution)/shard_map/jit(cholesky)/cholesky | solution.py:91
  891.7 11.7 %cholesky.181 = f32[128,128]{1,0:T(8,128)S(1)} custom-call(f32[128,128]{1,0:T(8,128)S(1)} %convolution_subtract_fusion.2), custom_call_target="Cholesky" | custom-call | tf_op jit(solution)/shard_map/jit(cholesky)/cholesky | solution.py:91
  906.1 4.2 while.17
  910.3 19.7 %custom-call.16 = f32[2,128,128]{1,2,0:T(8,128)S(1)} custom-call(f32[2,128,128]{2,1,0:T(8,128)S(1)} %get-tuple-element.150), custom_call_target="InvertDiagBlocksLowerTriangular" | custom-call | tf_op jit(solution)/shard_map/triangular_solve/custom-call.0 | solution.py:92
  930.9 8.6 fusion.16
  941.9 8.9 fusion.4
  (107 shorter events, 27.5 us)
Async XLA Ops:
  6.5 4.8 copy-start
  6.5 4.6 copy-start.8
  41.0 8.5 copy-start.9
  41.0 299.6 %all-to-all-start.1 = ((f32[16,2,8,128,128]{4,3,2,1,0:T(8,128)}), f32[16,2,8,128,128]{4,3,2,1,0:T(8,128)}, u32[]{:S(2)}, u32[]{:S(2)}) async-start(f32[16,2,8,128,128]{4,3,2,1,0:T(8,128)} %stack.2), calls=%async_computation.1 | async-start | bytes 33554432 | tf_op jit(solution)/shard_map/all_to_all | solution.py:55
  49.2 464.1 %all-reduce.14.cloned.1.call-start = ((), (), s32[]{:S(2)}) async-start(), calls=%async_computation.5 | async-start | bytes 15466496 | tf_op jit(solution)/shard_map/psum | solution.py:11
  372.4 208.6 %all-reduce.8.cloned.1.call-start = ((), (), s32[]{:S(2)}) async-start(), calls=%async_computation.2 | async-start | bytes 786432 | tf_op jit(solution)/shard_map/psum | solution.py:88
  513.3 3.3 copy-start.6
  516.9 3.1 copy-start.3
  520.8 278.8 %all-reduce.12.cloned.1.call-start = ((), (), s32[]{:S(2)}) async-start(), calls=%async_computation.4 | async-start | bytes 15466496 | tf_op jit(solution)/shard_map/psum | solution.py:11
  653.1 2.5 copy-start.2
  664.8 202.4 %all-reduce.10.cloned.1.call-start = ((), (), s32[]{:S(2)}) async-start(), calls=%async_computation.3 | async-start | bytes 786432 | tf_op jit(solution)/shard_map/psum | solution.py:88
  799.6 3.3 copy-start.7
  803.2 3.1 copy-start.4
  939.4 2.5 copy-start.5
  941.9 9.0 copy-start.1
Sparse Core Ops, SparseCore 0:
  372.5 140.7 all-reduce.13
  520.9 60.0 all-reduce.7
  664.9 134.6 all-reduce.11
  807.2 60.0 all-reduce.9
